TPU v7x, 32 devices: a whole 2x2x4 slice. The times are simulated.
32 devices in a mesh: face: 4 (over y, x), inface: 8 (over z, core).
Axes of the slice: x: 2, y: 2, z: 4, core: 2. Of those that a mesh axis runs over, the one named last changes fastest.
Arguments:
- model_state: float32 [4, 58, 131072], P(None, None, ('face', 'inface')), may hold values from -6 to 6
- coupling: float32 [58, 131072], P(None, ('face', 'inface')), may hold values from 0.05 to 20
- cosine: float32 [131072], P(('face', 'inface')), may hold values from 0.15 to 1
- albedo: float32 [131072], P(('face', 'inface')), may hold values from 0.05 to 0.8
- absorb: float32 [14], replicated, may hold values from 0.005 to 0.5
- weights: float32 [14], replicated, may hold values from 0.2 to 1.5
- span_map: int32 [4, 256], P('face', 'inface'), may hold values from 0 to 255, as said below
- sunlit: int32 [4, 256], P('face', 'inface'), may hold values from 0 to 1, as said below
Outputs:
- new_state: float32 [4, 58, 131072], P(None, None, ('face', 'inface'))
- surface_flux: float32 [131072], P(('face', 'inface'))
Inputs may be any that keep to these rules, and one draw needn't show every extreme that they name: `span_map`: in each face block the entries are a permutation of the spans; the blocks of one device go to each device of its face block exactly 4 at a time. The sunlit spans of a device and those of the device whose face index differs in bit 1 (same inface index) number 32 together; a device holds at most 28 sunlit spans, and some device exactly 28.
All inputs are finite; a program needn't handle non-finite values.
Results may differ from a plain program's by a relative error of at most 0.000023.
Values sent between devices are 32-bit elements; how exact they have to be, the bound alone decides.
A program may use at most 64 MiB of HBM per device.

v0:
```python
import functools
import math

import jax
import jax.numpy as jnp
from jax import lax
from jax.experimental import pallas as pl
from jax.experimental.pallas import tpu as pltpu
from jax.sharding import PartitionSpec as P

MESH = pl.DeviceIdType.MESH
LANES = 128


def exchange(count, axis, source, target, send_sem, recv_sem):
    me = lax.axis_index(axis)
    copies = []
    for k in range(1, count):
        peer = lax.rem(me + k, count)
        copy = pltpu.make_async_remote_copy(
            src_ref=source,
            dst_ref=target.at[me],
            send_sem=send_sem.at[k],
            recv_sem=recv_sem.at[k],
            device_id={axis: peer},
            device_id_type=MESH,
        )
        copy.start()
        copies.append(copy)
    return copies


def finish(count, axis, source, target, send_sem, recv_sem, copies):
    me = lax.axis_index(axis)
    for k in range(1, count):
        origin = lax.rem(me + count - k, count)
        pltpu.make_async_remote_copy(
            src_ref=source,
            dst_ref=target.at[origin],
            send_sem=send_sem.at[k],
            recv_sem=recv_sem.at[k],
            device_id={axis: origin},
            device_id_type=MESH,
        ).wait_recv()
    for copy in copies:
        copy.wait_send()


def greet(count, axis):
    me = lax.axis_index(axis)
    barrier = pltpu.get_barrier_semaphore()
    for k in range(1, count):
        pl.semaphore_signal(barrier, inc=1, device_id={axis: lax.rem(me + k, count)}, device_id_type=MESH)
    pl.semaphore_wait(barrier, count - 1)


def sky_kernel(count, spans, cosine, albedo, sunlit, span_map, gathered, packed, send_sem, recv_sem):
    me = lax.axis_index("inface")
    for s in range(spans):
        packed[pl.ds(s, 1), :] = cosine[pl.ds(s, 1), :] * sunlit[0, s].astype(jnp.float32)
    packed[pl.ds(spans, spans), :] = albedo[...]
    packed[pl.ds(2 * spans, 8), :] = jnp.full((8, LANES), -1.0, jnp.float32)
    packed[pl.ds(2 * spans, 1), pl.ds(0, spans)] = span_map[...].astype(jnp.float32)
    gathered[me] = packed[...]
    greet(count, "inface")
    copies = exchange(count, "inface", packed, gathered, send_sem, recv_sem)
    finish(count, "inface", packed, gathered, send_sem, recv_sem, copies)


def gather_sky(count, cosine, albedo, sunlit, span_map):
    spans = sunlit.shape[1]
    rows = 2 * spans + 8
    return pl.pallas_call(
        functools.partial(sky_kernel, count, spans),
        out_shape=jax.ShapeDtypeStruct((count, rows, LANES), jnp.float32),
        in_specs=[
            pl.BlockSpec(memory_space=pltpu.VMEM),
            pl.BlockSpec(memory_space=pltpu.VMEM),
            pl.BlockSpec(memory_space=pltpu.SMEM),
            pl.BlockSpec(memory_space=pltpu.VMEM),
        ],
        out_specs=pl.BlockSpec(memory_space=pltpu.VMEM),
        scratch_shapes=[
            pltpu.VMEM((rows, LANES), jnp.float32),
            pltpu.SemaphoreType.DMA((count,)),
            pltpu.SemaphoreType.DMA((count,)),
        ],
        compiler_params=pltpu.CompilerParams(collective_id=0, has_side_effects=True),
        name="gather_sky",
    )(cosine, albedo, sunlit, span_map)


def flux_kernel(count, spans, flux, sky, result, gathered, send_sem, recv_sem):
    me = lax.axis_index("inface")
    gathered[me] = flux[...]
    greet(count, "inface")
    copies = exchange(count, "inface", flux, gathered, send_sem, recv_sem)
    finish(count, "inface", flux, gathered, send_sem, recv_sem, copies)
    mine = (lax.broadcasted_iota(jnp.int32, (spans, spans), 0) + me * spans).astype(jnp.float32)
    total = jnp.zeros((spans, LANES), jnp.float32)
    for r in range(count):
        span_of = sky[r, pl.ds(2 * spans, 1), pl.ds(0, spans)]
        pick = jnp.where(mine == span_of, 1.0, 0.0)
        total = total + jnp.dot(
            pick, gathered[r], preferred_element_type=jnp.float32, precision=lax.Precision.HIGHEST
        )
    result[...] = total


def scatter_flux(count, flux, sky):
    spans = flux.shape[0]
    return pl.pallas_call(
        functools.partial(flux_kernel, count, spans),
        out_shape=jax.ShapeDtypeStruct(flux.shape, jnp.float32),
        in_specs=[pl.BlockSpec(memory_space=pltpu.VMEM)] * 2,
        out_specs=pl.BlockSpec(memory_space=pltpu.VMEM),
        scratch_shapes=[
            pltpu.VMEM((count, spans, LANES), jnp.float32),
            pltpu.SemaphoreType.DMA((count,)),
            pltpu.SemaphoreType.DMA((count,)),
        ],
        compiler_params=pltpu.CompilerParams(collective_id=1, has_side_effects=True),
        name="scatter_flux",
    )(flux, sky)


def column_kernel(
    span_map, absorb, weights, sky, state_in, coupling_in, state_out, flux, state, coupling, gain, depth, path,
    sun, in_sem, out_sem,
):
    fields, levels, blocks, _ = state.shape
    bands = absorb.shape[0]

    def columns(c):
        return pl.ds(c * LANES, LANES)

    for c in range(blocks):
        pltpu.make_async_copy(coupling_in.at[:, columns(c)], coupling.at[:, c, :], in_sem.at[0]).start()
        pltpu.make_async_copy(state_in.at[:, :, columns(c)], state.at[:, :, c, :], in_sem.at[1]).start()

    for e in range(blocks):
        span = span_map[0, e]
        owner, slot = span // blocks, span % blocks
        sun[0, pl.ds(e, 1), :] = sky[owner, pl.ds(slot, 1), :]
        sun[1, pl.ds(e, 1), :] = sky[owner, pl.ds(slot + blocks, 1), :]

    pltpu.make_async_copy(coupling, coupling, in_sem.at[0]).wait()
    pltpu.make_async_copy(state, state, in_sem.at[1]).wait()

    below = coupling[0]
    scale = 1.0 / (1.0 + below)
    gain_now = below * scale
    gain[0] = gain_now
    values = []
    for f in range(fields):
        value = state[f, 0] * scale
        state[f, 0] = value
        values.append(value)

    def eliminate(l, carry):
        above, gain_last, *last = carry
        below = coupling[l]
        scale = 1.0 / (1.0 + below + above - above * gain_last)
        gain_now = below * scale
        gain[l] = gain_now
        now = []
        for f in range(fields):
            value = (state[f, l] + above * last[f]) * scale
            state[f, l] = value
            now.append(value)
        return (below, gain_now, *now)

    carry = lax.fori_loop(1, levels, eliminate, (below, gain_now, *values), unroll=3)

    def substitute(k, carry):
        l = levels - 2 - k
        g = gain[l]
        now = []
        for f in range(fields):
            value = state[f, l] + g * carry[f]
            state[f, l] = value
            now.append(value)
        return tuple(now)

    lax.fori_loop(0, levels - 1, substitute, tuple(carry[2:]), unroll=3)

    for c in range(blocks):
        pltpu.make_async_copy(
            state.at[pl.ds(1, fields - 1), :, c, :], state_out.at[pl.ds(1, fields - 1), :, columns(c)], out_sem.at[0]
        ).start()

    cosine = sun[0]
    lit = cosine > 0.0
    slant = (-math.log2(math.e)) / jnp.where(lit, cosine, 1.0)

    def optics(l, total):
        step = (1.2 + jnp.tanh(state[1, l])) * slant
        depth[l] = step
        path[l] = total
        return total + step

    whole = lax.fori_loop(0, levels, optics, jnp.zeros_like(slant), unroll=2)
    path[levels] = whole

    for g in range(blocks // 8):
        rows = pl.ds(g * 8, 8)
        shape = (8, LANES)
        coefficient = [jnp.full(shape, absorb[b], jnp.float32) for b in range(bands)]
        weight = [jnp.full(shape, 0.3 * weights[b], jnp.float32) for b in range(bands)]
        surface = sun[1, rows, :]
        sun_rows = sun[0, rows, :]
        bottom = path[levels, rows, :]
        ups = []
        sum_up = jnp.zeros(shape, jnp.float32)
        sum_down = jnp.zeros(shape, jnp.float32)
        for b in range(bands):
            down = weight[b] * jnp.exp2(coefficient[b] * bottom)
            up = surface * (down * (1.0 / 0.3))
            ups.append(up)
            sum_up = sum_up + up
            sum_down = sum_down + down
        flux[rows, :] = (1.0 - surface) * sun_rows * (sum_down * (1.0 / 0.3))
        net = sum_up - sum_down * (1.0 / 0.3)
        factor = 5.0 * sun_rows

        def radiate(k, carry):
            l = levels - 1 - k
            net_below, *ups = carry
            step = depth[l, rows, :]
            above = path[l, rows, :]
            sum_up = [None, None]
            sum_down = [None, None]
            now = []
            for b in range(bands):
                passed = jnp.exp2(coefficient[b] * step)
                down = weight[b] * jnp.exp2(coefficient[b] * above)
                up = (ups[b] - down) * passed + down
                now.append(up)
                h = b % 2
                sum_up[h] = up if sum_up[h] is None else sum_up[h] + up
                sum_down[h] = down if sum_down[h] is None else sum_down[h] + down
            net = (sum_up[0] + sum_up[1]) - (sum_down[0] + sum_down[1]) * (1.0 / 0.3)
            state[0, l, rows, :] = state[0, l, rows, :] + factor * (net_below - net)
            return (net, *now)

        lax.fori_loop(0, levels, radiate, (net, *ups), unroll=2)
        for c in range(g * 8, g * 8 + 8):
            pltpu.make_async_copy(state.at[0, :, c, :], state_out.at[0, :, columns(c)], out_sem.at[1]).start()

    pltpu.make_async_copy(state.at[pl.ds(1, fields - 1)], state.at[pl.ds(1, fields - 1)], out_sem.at[0]).wait()
    pltpu.make_async_copy(state.at[0], state.at[0], out_sem.at[1]).wait()


def run_columns(span_map, absorb, weights, sky, model_state, coupling):
    fields, levels, columns = model_state.shape
    blocks = columns // LANES
    smem = pl.BlockSpec(memory_space=pltpu.SMEM)
    return pl.pallas_call(
        column_kernel,
        out_shape=(
            jax.ShapeDtypeStruct(model_state.shape, jnp.float32),
            jax.ShapeDtypeStruct((blocks, LANES), jnp.float32),
        ),
        in_specs=[
            smem,
            smem,
            smem,
            pl.BlockSpec(memory_space=pltpu.VMEM),
            pl.BlockSpec(memory_space=pl.ANY),
            pl.BlockSpec(memory_space=pl.ANY),
        ],
        out_specs=(pl.BlockSpec(memory_space=pl.ANY), pl.BlockSpec(memory_space=pltpu.VMEM)),
        scratch_shapes=[
            pltpu.VMEM((fields, levels, blocks, LANES), jnp.float32),
            pltpu.VMEM((levels, blocks, LANES), jnp.float32),
            pltpu.VMEM((levels, blocks, LANES), jnp.float32),
            pltpu.VMEM((levels, blocks, LANES), jnp.float32),
            pltpu.VMEM((levels + 1, blocks, LANES), jnp.float32),
            pltpu.VMEM((2, blocks, LANES), jnp.float32),
            pltpu.SemaphoreType.DMA((2,)),
            pltpu.SemaphoreType.DMA((2,)),
        ],
        compiler_params=pltpu.CompilerParams(vmem_limit_bytes=24 * 1024 * 1024),
        name="columns",
    )(span_map, absorb, weights, sky, model_state, coupling)


def body(model_state, coupling, cosine, albedo, absorb, weights, span_map, sunlit):
    count = lax.axis_size("inface")
    spans = span_map.shape[1]
    sky = gather_sky(count, cosine.reshape(spans, LANES), albedo.reshape(spans, LANES), sunlit, span_map)
    new_state, flux = run_columns(span_map, absorb, weights, sky, model_state, coupling)
    surface = scatter_flux(count, flux, sky)
    return new_state, surface.reshape(cosine.shape)


def solution(mesh):
    in_specs = (
        P(None, None, ("face", "inface")),
        P(None, ("face", "inface")),
        P(("face", "inface")),
        P(("face", "inface")),
        P(),
        P(),
        P("face", "inface"),
        P("face", "inface"),
    )
    out_specs = (P(None, None, ("face", "inface")), P(("face", "inface")))
    return jax.shard_map(body, mesh=mesh, in_specs=in_specs, out_specs=out_specs, check_vma=False)
```

profile of v0, /device:TPU:0, one launch (start us, length us, event | category | flops | bytes accessed | tf_op | source)
XLA Modules:
  0.0 55.1 jit_solution(6897856304640033272)
XLA Ops:
  0.6 0.0 copy-start.4
  0.6 0.0 copy-start.6
  0.7 0.0 copy-start.5
  0.7 0.0 copy-start.2
  0.7 12.2 %gather_sky.1.sky = f32[8,72,128]{2,1,0:T(8,128)} custom-call(f32[32,128]{1,0:T(8,128)} %bitcast.4, f32[32,128]{1,0:T(8,128)} %bitcast.5, s32[1,32]{1,0:T(1,128)} %sunlit.1, s32[1,32]{1,0:T(1,128)} %span_map.3), custom_call_target="tpu_custom_call" | custom-call | tf_op jit(solution)/shard_map/gather_sky/pallas_call | solution.py:73
  12.9 0.0 copy-start.1
  12.9 4.3 %copy.10.state_in = f32[4,58,4096]{2,1,0:T(8,128)S(1)} copy(f32[4,58,4096]{2,0,1:T(4,128)} %param.8) | data formatting | bytes 7602176 | tf_op args[0]
  17.3 0.0 copy-done.4
  17.3 0.0 copy-done.6
  17.3 0.0 copy-done.5
  17.3 0.0 copy-done.2
  17.3 0.0 copy-done.1
  17.3 18.5 %columns.1 = (f32[4,58,4096]{2,1,0:T(8,128)S(1)}, f32[32,128]{1,0:T(8,128)S(1)}) custom-call(s32[1,32]{1,0:T(1,128)S(1)} %copy-done.4, f32[14]{0:T(128)S(1)} %copy-done.5, f32[14]{0:T(128)S(1)} %copy-done.6, f32[8,72,128]{2,1,0:T(8,128)S(1)} %copy-done.1, f32[4,58,4096]{2,1,0:T(8,128)S(1)} %copy.10.state_in, f32[58,4096]{1,0:T(8,128)S(1)} %copy-done.2), custom_call_target="tpu_custom_call" | custom-call | tf_op jit(solution)/shard_map/columns/pallas_call | solution.py:258
  35.8 0.0 copy-start
  35.8 1.9 %copy-done = f32[4,58,4096]{2,1,0:T(8,128)} copy-done((f32[4,58,4096]{2,1,0:T(8,128)}, f32[4,58,4096]{2,1,0:T(8,128)S(1)}, u32[]{:S(2)}) %copy-start) | copy-done | bytes 3801112
  37.7 0.0 copy-start.3
  37.7 0.6 %copy-done.3 = f32[32,128]{1,0:T(8,128)} copy-done((f32[32,128]{1,0:T(8,128)}, f32[32,128]{1,0:T(8,128)S(1)}, u32[]{:S(2)}) %copy-start.3) | copy-done | bytes 16408
  38.3 9.6 %scatter_flux.1 = f32[32,128]{1,0:T(8,128)} custom-call(f32[32,128]{1,0:T(8,128)} %copy-done.3, f32[8,72,128]{2,1,0:T(8,128)} %gather_sky.1.sky), custom_call_target="tpu_custom_call" | custom-call | tf_op jit(solution)/shard_map/scatter_flux/pallas_call | solution.py:112
  47.9 0.0 copy-start.7
  48.0 6.5 %copy.11 = f32[4,58,4096]{2,0,1:T(4,128)} copy(f32[4,58,4096]{2,1,0:T(8,128)} %copy-done) | data formatting | bytes 7602176
  54.5 0.0 copy-done.7
  54.5 0.6 %copy.13 = f32[4096]{0:T(1024)} copy(f32[4096]{0:T(1024)S(1)} %bitcast.3) | data formatting | bytes 32768
Async XLA Ops:
  0.6 16.6 %copy-start.4 = (s32[1,32]{1,0:T(1,128)S(1)}, s32[1,32]{1,0:T(1,128)}, u32[]{:S(2)}) copy-start(s32[1,32]{1,0:T(1,128)} %span_map.3) | copy-start | bytes 388
  0.6 16.6 %copy-start.6 = (f32[14]{0:T(128)S(1)}, f32[14]{0:T(128)}, u32[]{:S(2)}) copy-start(f32[14]{0:T(128)} %weights.1) | copy-start | bytes 172
  0.7 16.6 %copy-start.5 = (f32[14]{0:T(128)S(1)}, f32[14]{0:T(128)}, u32[]{:S(2)}) copy-start(f32[14]{0:T(128)} %absorb.1) | copy-start | bytes 172
  0.7 16.6 %copy-start.2 = (f32[58,4096]{1,0:T(8,128)S(1)}, f32[58,4096]{1,0:T(8,128)}, u32[]{:S(2)}) copy-start(f32[58,4096]{1,0:T(8,128)} %coupling_in.1) | copy-start | bytes 2850820
  12.9 4.4 %copy-start.1 = (f32[8,72,128]{2,1,0:T(8,128)S(1)}, f32[8,72,128]{2,1,0:T(8,128)}, u32[]{:S(2)}) copy-start(f32[8,72,128]{2,1,0:T(8,128)} %gather_sky.1.sky) | copy-start | bytes 884740
  35.8 1.9 %copy-start = (f32[4,58,4096]{2,1,0:T(8,128)}, f32[4,58,4096]{2,1,0:T(8,128)S(1)}, u32[]{:S(2)}) copy-start(f32[4,58,4096]{2,1,0:T(8,128)S(1)} %get-tuple-element.6) | copy-start | bytes 11403268
  37.7 0.6 %copy-start.3 = (f32[32,128]{1,0:T(8,128)}, f32[32,128]{1,0:T(8,128)S(1)}, u32[]{:S(2)}) copy-start(f32[32,128]{1,0:T(8,128)S(1)} %get-tuple-element.5.flux) | copy-start | bytes 49156
  47.9 6.5 %copy-start.7 = (f32[32,128]{1,0:T(8,128)S(1)}, f32[32,128]{1,0:T(8,128)}, u32[]{:S(2)}) copy-start(f32[32,128]{1,0:T(8,128)} %scatter_flux.1) | copy-start | bytes 49156
where the time goes:
time: 55.3 us; the launch traced here: 55.1 us
  Pallas kernels  40.3 us (73%)
  local copies, waits for them, and re-layouts  14 us (25%)
  between operations  0.76 us (1%)
    pallas_call x1, Pallas kernels, run_columns(): pl.pallas_call(column_kernel, out_shape=(jax.ShapeDtypeStruct(model_state...  18.5 us
    unnamed x19, local copies, waits for them, and re-layouts  14 us
    pallas_call x1, Pallas kernels, gather_sky(): pl.pallas_call(functools.partial(sky_kernel, count, spans), out_shape=jax...  12.2 us
    pallas_call x1, Pallas kernels, scatter_flux(): pl.pallas_call(functools.partial(flux_kernel, count, spans), out_shape=ja...  9.61 us

commit v1 on v0

v1 whole, which is shorter than its diff:
```python
import functools
import math

import jax
import jax.numpy as jnp
from jax import lax
from jax.experimental import pallas as pl
from jax.experimental.pallas import tpu as pltpu
from jax.sharding import PartitionSpec as P

MESH = pl.DeviceIdType.MESH
LANES = 128


def exchange(count, axis, source, target, send_sem, recv_sem):
    me = lax.axis_index(axis)
    copies = []
    for k in range(1, count):
        peer = lax.rem(me + k, count)
        copy = pltpu.make_async_remote_copy(
            src_ref=source,
            dst_ref=target.at[me],
            send_sem=send_sem.at[k],
            recv_sem=recv_sem.at[k],
            device_id={axis: peer},
            device_id_type=MESH,
        )
        copy.start()
        copies.append(copy)
    return copies


def finish(count, axis, source, target, send_sem, recv_sem, copies):
    me = lax.axis_index(axis)
    for k in range(1, count):
        origin = lax.rem(me + count - k, count)
        pltpu.make_async_remote_copy(
            src_ref=source,
            dst_ref=target.at[origin],
            send_sem=send_sem.at[k],
            recv_sem=recv_sem.at[k],
            device_id={axis: origin},
            device_id_type=MESH,
        ).wait_recv()
    for copy in copies:
        copy.wait_send()


def greet(count, axis):
    me = lax.axis_index(axis)
    barrier = pltpu.get_barrier_semaphore()
    for k in range(1, count):
        pl.semaphore_signal(barrier, inc=1, device_id={axis: lax.rem(me + k, count)}, device_id_type=MESH)
    pl.semaphore_wait(barrier, count - 1)


SKIP = ()


def step_kernel(
    count, cosine, albedo, sunlit, span_map, span_row, absorb, weights, state_in, coupling_in, state_out, surface_out,
    state, partial, coupling, gain, depth, path, sun, packed, sky, flux, fluxes, in_sem, out_sem, send_sem, recv_sem,
):
    fields, levels, blocks, _ = partial.shape
    bands = absorb.shape[0]
    me = lax.axis_index("inface") if count > 1 else 0

    def columns(c):
        return pl.ds(c * LANES, LANES)

    def field(f, first=0, size=blocks):
        return pl.ds(first * fields + f, size, stride=fields)

    for c in range(blocks):
        pltpu.make_async_copy(coupling_in.at[:, columns(c)], coupling.at[:, c, :], in_sem.at[0]).start()
    for c in range(blocks):
        pltpu.make_async_copy(state_in.at[:, :, columns(c)], state.at[:, pl.ds(c * fields, fields), :], in_sem.at[1]).start()

    for s in range(blocks):
        packed[pl.ds(s, 1), :] = cosine[pl.ds(s, 1), :] * sunlit[0, s].astype(jnp.float32)
    packed[pl.ds(blocks, blocks), :] = albedo[...]
    packed[pl.ds(2 * blocks, 8), :] = jnp.full((8, LANES), -1.0, jnp.float32)
    packed[pl.ds(2 * blocks, 1), pl.ds(0, blocks)] = span_row[...].astype(jnp.float32)
    sky[me] = packed[...]
    if count > 1:
        greet(count, "inface")
    sky_copies = exchange(count, "inface", packed, sky, send_sem.at[0], recv_sem.at[0]) if count > 1 else []

    pltpu.make_async_copy(coupling, coupling, in_sem.at[0]).wait()
    pltpu.make_async_copy(state, state, in_sem.at[1]).wait()

    if "solve" not in SKIP:
        below = coupling[0]
        scale = 1.0 / (1.0 + below)
        gain_now = below * scale
        gain[0] = gain_now
        values = []
        for f in range(fields):
            value = state[0, field(f), :] * scale
            partial[f, 0] = value
            values.append(value)

        def eliminate(l, carry):
            above, gain_last, *last = carry
            below = coupling[l]
            scale = 1.0 / (1.0 + below + above - above * gain_last)
            gain_now = below * scale
            gain[l] = gain_now
            now = []
            for f in range(fields):
                value = (state[l, field(f), :] + above * last[f]) * scale
                partial[f, l] = value
                now.append(value)
            return (below, gain_now, *now)

        carry = lax.fori_loop(1, levels, eliminate, (below, gain_now, *values), unroll=3)
        for f in range(fields):
            state[levels - 1, field(f), :] = carry[2 + f]

        def substitute(k, carry):
            l = levels - 2 - k
            g = gain[l]
            now = []
            for f in range(fields):
                value = partial[f, l] + g * carry[f]
                state[l, field(f), :] = value
                now.append(value)
            return tuple(now)

        lax.fori_loop(0, levels - 1, substitute, tuple(carry[2:]), unroll=3)

    if count > 1:
        finish(count, "inface", packed, sky, send_sem.at[0], recv_sem.at[0], sky_copies)
    for e in range(blocks):
        span = span_map[0, e]
        owner, slot = span // blocks, span % blocks
        sun[0, pl.ds(e, 1), :] = sky[owner, pl.ds(slot, 1), :]
        sun[1, pl.ds(e, 1), :] = sky[owner, pl.ds(slot + blocks, 1), :]

    cosine_here = sun[0]
    slant = (-math.log2(math.e)) / jnp.where(cosine_here > 0.0, cosine_here, 1.0)

    def optics(l, total):
        step = (1.2 + jnp.tanh(state[l, field(1), :])) * slant
        depth[l] = step
        path[l] = total
        return total + step

    if "optics" not in SKIP:
        bottom = lax.fori_loop(0, levels, optics, jnp.zeros_like(slant), unroll=2)
        path[levels] = bottom
    else:
        bottom = slant

    shape = (8, LANES)
    for g in range(blocks // 8):
        rows = pl.ds(g * 8, 8)
        total = jnp.zeros(shape, jnp.float32)
        for b in range(bands):
            total = total + weights[b] * jnp.exp2(absorb[b] * path[levels, rows, :])
        flux[rows, :] = (1.0 - sun[1, rows, :]) * sun[0, rows, :] * total
    fluxes[me] = flux[...]
    flux_copies = exchange(count, "inface", flux, fluxes, send_sem.at[1], recv_sem.at[1]) if count > 1 else []

    for g in range(blocks // 8):
        rows = pl.ds(g * 8, 8)
        coefficient = [jnp.full(shape, absorb[b], jnp.float32) for b in range(bands)]
        weight = [jnp.full(shape, 0.3 * weights[b], jnp.float32) for b in range(bands)]
        reflected = sun[1, rows, :] * (1.0 / 0.3)
        low = path[levels, rows, :]
        ups = []
        sum_up = jnp.zeros(shape, jnp.float32)
        sum_down = jnp.zeros(shape, jnp.float32)
        for b in range(bands):
            down = weight[b] * jnp.exp2(coefficient[b] * low)
            up = reflected * down
            ups.append(up)
            sum_up = sum_up + up
            sum_down = sum_down + down
        net = sum_up - sum_down * (1.0 / 0.3)
        factor = 5.0 * sun[0, rows, :]

        def radiate(k, carry):
            l = levels - 1 - k
            net_below, *ups = carry
            step = depth[l, rows, :]
            above = path[l, rows, :]
            sum_up = [None, None]
            sum_down = [None, None]
            now = []
            for b in range(bands):
                passed = jnp.exp2(coefficient[b] * step)
                down = weight[b] * jnp.exp2(coefficient[b] * above)
                up = (ups[b] - down) * passed + down
                now.append(up)
                h = b % 2
                sum_up[h] = up if sum_up[h] is None else sum_up[h] + up
                sum_down[h] = down if sum_down[h] is None else sum_down[h] + down
            net = (sum_up[0] + sum_up[1]) - (sum_down[0] + sum_down[1]) * (1.0 / 0.3)
            here = field(0, g * 8, 8)
            state[l, here, :] = state[l, here, :] + factor * (net_below - net)
            return (net, *now)

        if "radiate" not in SKIP:
            lax.fori_loop(0, levels, radiate, (net, *ups), unroll=2)
        for c in range(g * 8, g * 8 + 8):
            pltpu.make_async_copy(state.at[:, pl.ds(c * fields, fields), :], state_out.at[:, :, columns(c)], out_sem.at[0]).start()

    if count > 1:
        finish(count, "inface", flux, fluxes, send_sem.at[1], recv_sem.at[1], flux_copies)
    mine = (lax.broadcasted_iota(jnp.int32, (blocks, blocks), 0) + me * blocks).astype(jnp.float32)
    surface = jnp.zeros((blocks, LANES), jnp.float32)
    for r in range(count):
        span_of = sky[r, pl.ds(2 * blocks, 1), pl.ds(0, blocks)]
        pick = jnp.where(mine == span_of, 1.0, 0.0)
        surface = surface + jnp.dot(
            pick, fluxes[r], preferred_element_type=jnp.float32, precision=lax.Precision.HIGHEST
        )
    surface_out[...] = surface
    pltpu.make_async_copy(state, state, out_sem.at[0]).wait()


def run_step(count, cosine, albedo, sunlit, span_map, absorb, weights, model_state, coupling):
    levels, fields, columns = model_state.shape
    blocks = columns // LANES
    smem = pl.BlockSpec(memory_space=pltpu.SMEM)
    vmem = pl.BlockSpec(memory_space=pltpu.VMEM)
    anywhere = pl.BlockSpec(memory_space=pl.ANY)
    rows = 2 * blocks + 8
    return pl.pallas_call(
        functools.partial(step_kernel, count),
        out_shape=(
            jax.ShapeDtypeStruct(model_state.shape, jnp.float32),
            jax.ShapeDtypeStruct((blocks, LANES), jnp.float32),
        ),
        in_specs=[vmem, vmem, smem, smem, vmem, smem, smem, anywhere, anywhere],
        out_specs=(anywhere, vmem),
        scratch_shapes=[
            pltpu.VMEM((levels, blocks * fields, LANES), jnp.float32),
            pltpu.VMEM((fields, levels, blocks, LANES), jnp.float32),
            pltpu.VMEM((levels, blocks, LANES), jnp.float32),
            pltpu.VMEM((levels, blocks, LANES), jnp.float32),
            pltpu.VMEM((levels, blocks, LANES), jnp.float32),
            pltpu.VMEM((levels + 1, blocks, LANES), jnp.float32),
            pltpu.VMEM((2, blocks, LANES), jnp.float32),
            pltpu.VMEM((rows, LANES), jnp.float32),
            pltpu.VMEM((count, rows, LANES), jnp.float32),
            pltpu.VMEM((blocks, LANES), jnp.float32),
            pltpu.VMEM((count, blocks, LANES), jnp.float32),
            pltpu.SemaphoreType.DMA((2,)),
            pltpu.SemaphoreType.DMA((1,)),
            pltpu.SemaphoreType.DMA((2, max(count, 2))),
            pltpu.SemaphoreType.DMA((2, max(count, 2))),
        ],
        compiler_params=pltpu.CompilerParams(
            collective_id=0 if count > 1 else None, has_side_effects=True, vmem_limit_bytes=40 * 1024 * 1024
        ),
        name="step",
    )(cosine, albedo, sunlit, span_map, span_map, absorb, weights, model_state, coupling)


def body(model_state, coupling, cosine, albedo, absorb, weights, span_map, sunlit):
    count = lax.axis_size("inface")
    spans = span_map.shape[1]
    new_state, surface = run_step(
        count,
        cosine.reshape(spans, LANES),
        albedo.reshape(spans, LANES),
        sunlit,
        span_map,
        absorb,
        weights,
        model_state.transpose(1, 0, 2),
        coupling,
    )
    return new_state.transpose(1, 0, 2), surface.reshape(cosine.shape)


def solution(mesh):
    in_specs = (
        P(None, None, ("face", "inface")),
        P(None, ("face", "inface")),
        P(("face", "inface")),
        P(("face", "inface")),
        P(),
        P(),
        P("face", "inface"),
        P("face", "inface"),
    )
    out_specs = (P(None, None, ("face", "inface")), P(("face", "inface")))
    return jax.shard_map(body, mesh=mesh, in_specs=in_specs, out_specs=out_specs, check_vma=False)
```

time: 55.3 us -> 32.9 us (0.59)
  Pallas kernels: 40.3 us -> 21.9 us
  local copies, waits for them, and re-layouts: 14 us -> 9.83 us
    pallas_call x3 -> x1, Pallas kernels: 40.3 us -> 21.9 us  [run_step(): pl.pallas_call(functools.partial(step_kernel, count), out_shape=(jax.Shap...]
    unnamed x19 -> x18, local copies, waits for them, and re-layouts: 14 us -> 9.83 us
where the time goes in v1:
time: 32.9 us; the launch traced here: 32.4 us
  Pallas kernels  21.9 us (67%)
  local copies, waits for them, and re-layouts  9.83 us (30%)
  between operations  0.66 us (2%)
    pallas_call x1, Pallas kernels, run_step(): pl.pallas_call(functools.partial(step_kernel, count), out_shape=(jax.Shap...  21.9 us
    unnamed x18, local copies, waits for them, and re-layouts  9.83 us

profile of v1, /device:TPU:0, one launch (start us, length us, event | category | flops | bytes accessed | tf_op | source)
XLA Modules:
  0.0 32.4 jit_solution(12652737653273571118)
XLA Ops:
  0.6 0.0 copy-start
  0.6 2.1 %copy-done = f32[4,58,4096]{2,0,1:T(4,128)S(1)} copy-done((f32[4,58,4096]{2,0,1:T(4,128)S(1)}, f32[4,58,4096]{2,0,1:T(4,128)}, u32[]{:S(2)}) %copy-start) | copy-done | bytes 3801112
  2.7 0.0 copy-start.1
  2.7 1.2 %copy-done.1 = f32[58,4096]{1,0:T(8,128)S(1)} copy-done((f32[58,4096]{1,0:T(8,128)S(1)}, f32[58,4096]{1,0:T(8,128)}, u32[]{:S(2)}) %copy-start.1) | copy-done | bytes 950296
  3.9 0.0 copy-start.2
  3.9 0.7 %copy-done.2 = f32[4096]{0:T(1024)S(1)} copy-done((f32[4096]{0:T(1024)S(1)}, f32[4096]{0:T(1024)}, u32[]{:S(2)}) %copy-start.2) | copy-done | bytes 16408
  4.7 0.0 copy-start.3
  4.7 0.7 %copy-done.3 = f32[4096]{0:T(1024)S(1)} copy-done((f32[4096]{0:T(1024)S(1)}, f32[4096]{0:T(1024)}, u32[]{:S(2)}) %copy-start.3) | copy-done | bytes 16408
  5.4 0.0 copy-start.4
  5.4 0.7 %copy-done.4 = s32[1,32]{1,0:T(1,128)S(1)} copy-done((s32[1,32]{1,0:T(1,128)S(1)}, s32[1,32]{1,0:T(1,128)}, u32[]{:S(2)}) %copy-start.4) | copy-done | bytes 152
  6.0 0.0 copy-start.5
  6.0 0.7 %copy-done.5 = s32[1,32]{1,0:T(1,128)S(1)} copy-done((s32[1,32]{1,0:T(1,128)S(1)}, s32[1,32]{1,0:T(1,128)}, u32[]{:S(2)}) %copy-start.5) | copy-done | bytes 152
  6.7 0.0 copy-start.6
  6.7 0.7 %copy-done.6 = f32[14]{0:T(128)S(1)} copy-done((f32[14]{0:T(128)S(1)}, f32[14]{0:T(128)}, u32[]{:S(2)}) %copy-start.6) | copy-done | bytes 80
  7.3 0.0 copy-start.7
  7.3 0.7 %copy-done.7 = f32[14]{0:T(128)S(1)} copy-done((f32[14]{0:T(128)S(1)}, f32[14]{0:T(128)}, u32[]{:S(2)}) %copy-start.7) | copy-done | bytes 80
  8.0 21.9 %step.1 = (f32[58,4,4096]{2,1,0:T(4,128)S(1)}, f32[32,128]{1,0:T(8,128)S(1)}) custom-call(f32[32,128]{1,0:T(8,128)S(1)} %bitcast.7, f32[32,128]{1,0:T(8,128)S(1)} %bitcast.8, s32[1,32]{1,0:T(1,128)S(1)} %copy-done.5, s32[1,32]{1,0:T(1,128)S(1)} %copy-done.4, s32[1,32]{1,0:T(1,128)S(1)} %copy-done.4, f32[14]{0:T(128)S(1)} %copy-done.6, f32[14]{0:T(128)S(1)} %copy-done.7, ...), custom_call_target="tpu_custom_call" | custom-call | tf_op jit(solution)/shard_map/step/pallas_call | solution.py:230
  29.9 1.9 %copy.12 = f32[4,58,4096]{2,0,1:T(4,128)} copy(f32[4,58,4096]{2,0,1:T(4,128)S(1)} %bitcast.6) | data formatting | bytes 7602176
  31.8 0.6 %copy.13 = f32[4096]{0:T(1024)} copy(f32[4096]{0:T(1024)S(1)} %bitcast.9) | data formatting | bytes 32768
Async XLA Ops:
  0.6 2.1 %copy-start = (f32[4,58,4096]{2,0,1:T(4,128)S(1)}, f32[4,58,4096]{2,0,1:T(4,128)}, u32[]{:S(2)}) copy-start(f32[4,58,4096]{2,0,1:T(4,128)} %param.8) | copy-start | bytes 11403268
  2.7 1.2 %copy-start.1 = (f32[58,4096]{1,0:T(8,128)S(1)}, f32[58,4096]{1,0:T(8,128)}, u32[]{:S(2)}) copy-start(f32[58,4096]{1,0:T(8,128)} %coupling_in.1) | copy-start | bytes 2850820
  3.9 0.7 %copy-start.2 = (f32[4096]{0:T(1024)S(1)}, f32[4096]{0:T(1024)}, u32[]{:S(2)}) copy-start(f32[4096]{0:T(1024)} %param.10) | copy-start | bytes 49156
  4.7 0.7 %copy-start.3 = (f32[4096]{0:T(1024)S(1)}, f32[4096]{0:T(1024)}, u32[]{:S(2)}) copy-start(f32[4096]{0:T(1024)} %param.11) | copy-start | bytes 49156
  5.4 0.7 %copy-start.4 = (s32[1,32]{1,0:T(1,128)S(1)}, s32[1,32]{1,0:T(1,128)}, u32[]{:S(2)}) copy-start(s32[1,32]{1,0:T(1,128)} %span_row.1) | copy-start | bytes 388
  6.0 0.7 %copy-start.5 = (s32[1,32]{1,0:T(1,128)S(1)}, s32[1,32]{1,0:T(1,128)}, u32[]{:S(2)}) copy-start(s32[1,32]{1,0:T(1,128)} %sunlit.1) | copy-start | bytes 388
  6.7 0.7 %copy-start.6 = (f32[14]{0:T(128)S(1)}, f32[14]{0:T(128)}, u32[]{:S(2)}) copy-start(f32[14]{0:T(128)} %absorb.1) | copy-start | bytes 172
  7.3 0.7 %copy-start.7 = (f32[14]{0:T(128)S(1)}, f32[14]{0:T(128)}, u32[]{:S(2)}) copy-start(f32[14]{0:T(128)} %weights.1) | copy-start | bytes 172

commit v2 on v1

--- a/solution.py
+++ b/solution.py
@@ -51,18 +51,54 @@
     barrier = pltpu.get_barrier_semaphore()
     for k in range(1, count):
         pl.semaphore_signal(barrier, inc=1, device_id={axis: lax.rem(me + k, count)}, device_id_type=MESH)
-    pl.semaphore_wait(barrier, count - 1)
+
+
+def greeted(count):
+    pl.semaphore_wait(pltpu.get_barrier_semaphore(), count - 1)
+
+
+def sky_copy(axis, source, target, owner, peer, send_sem, recv_sem, k):
+    return pltpu.make_async_remote_copy(
+        src_ref=source,
+        dst_ref=target.at[owner],
+        send_sem=send_sem.at[k],
+        recv_sem=recv_sem.at[k],
+        device_id={axis: peer},
+        device_id_type=MESH,
+    )
 
 
 SKIP = ()
 
 
 def step_kernel(
-    count, cosine, albedo, sunlit, span_map, span_row, absorb, weights, state_in, coupling_in, state_out, surface_out,
-    state, partial, coupling, gain, depth, path, sun, packed, sky, flux, fluxes, in_sem, out_sem, send_sem, recv_sem,
+    count, cosine_in, albedo_in, sunlit_in, span_map_in, absorb_in, weights_in, state_in, coupling_in,
+    state_out, surface_out,
+    span_row, sunlit, span_map, absorb, weights,
+    state, partial, coupling, gain, depth, path, sun, packed, sky, flux, fluxes,
+    in_sem, small_sem, out_sem, sky_send, sky_recv, pass_send, pass_recv, send_sem, recv_sem,
 ):
     fields, levels, blocks, _ = partial.shape
     bands = absorb.shape[0]
+    chips = count // 2
+    if count > 1:
+        greet(count, "inface")
+    small = [
+        pltpu.make_async_copy(source, target, small_sem.at[i])
+        for i, (source, target) in enumerate(
+            [
+                (cosine_in, packed.at[pl.ds(0, blocks)]),
+                (albedo_in, packed.at[pl.ds(blocks, blocks)]),
+                (sunlit_in, sunlit),
+                (span_map_in, span_map),
+                (span_map_in, span_row),
+                (absorb_in, absorb),
+                (weights_in, weights),
+            ]
+        )
+    ]
+    for copy in small:
+        copy.start()
     me = lax.axis_index("inface") if count > 1 else 0
 
     def columns(c):
@@ -76,15 +112,23 @@
     for c in range(blocks):
         pltpu.make_async_copy(state_in.at[:, :, columns(c)], state.at[:, pl.ds(c * fields, fields), :], in_sem.at[1]).start()
 
+    for copy in small:
+        copy.wait()
     for s in range(blocks):
-        packed[pl.ds(s, 1), :] = cosine[pl.ds(s, 1), :] * sunlit[0, s].astype(jnp.float32)
-    packed[pl.ds(blocks, blocks), :] = albedo[...]
-    packed[pl.ds(2 * blocks, 8), :] = jnp.full((8, LANES), -1.0, jnp.float32)
-    packed[pl.ds(2 * blocks, 1), pl.ds(0, blocks)] = span_row[...].astype(jnp.float32)
+        packed[pl.ds(s, 1), :] = packed[pl.ds(s, 1), :] * sunlit[0, s].astype(jnp.float32)
+    flux[pl.ds(blocks, 8), :] = jnp.full((8, LANES), -1.0, jnp.float32)
+    flux[pl.ds(blocks, 1), pl.ds(0, blocks)] = span_row[...].astype(jnp.float32)
     sky[me] = packed[...]
-    if count > 1:
-        greet(count, "inface")
-    sky_copies = exchange(count, "inface", packed, sky, send_sem.at[0], recv_sem.at[0]) if count > 1 else []
+    sky_copies = []
+    if count > 1:
+        greeted(count)
+        sibling = me + 1 - 2 * lax.rem(me, 2)
+        for k in range(1, chips):
+            peer = lax.rem(me + 2 * k, count)
+            sky_copies.append(sky_copy("inface", packed, sky, me, peer, sky_send, sky_recv, k))
+        sky_copies.append(sky_copy("inface", packed, sky, me, sibling, sky_send, sky_recv, 0))
+        for copy in sky_copies:
+            copy.start()
 
     pltpu.make_async_copy(coupling, coupling, in_sem.at[0]).wait()
     pltpu.make_async_copy(state, state, in_sem.at[1]).wait()
@@ -130,7 +174,26 @@
         lax.fori_loop(0, levels - 1, substitute, tuple(carry[2:]), unroll=3)
 
     if count > 1:
-        finish(count, "inface", packed, sky, send_sem.at[0], recv_sem.at[0], sky_copies)
+        for k in range(1, chips):
+            origin = lax.rem(me + count - 2 * k, count)
+            sky_copy("inface", packed, sky, origin, origin, sky_send, sky_recv, k).wait_recv()
+            copy = sky_copy("inface", sky.at[origin], sky, origin, sibling, pass_send, pass_recv, k)
+            copy.start()
+            sky_copies.append(copy)
+
+    def optics(l, nothing):
+        depth[l] = 1.2 + jnp.tanh(state[l, field(1), :])
+        return nothing
+
+    lax.fori_loop(0, levels, optics, 0, unroll=2)
+
+    if count > 1:
+        sky_copy("inface", packed, sky, sibling, sibling, sky_send, sky_recv, 0).wait_recv()
+        for k in range(1, chips):
+            origin = lax.rem(sibling + count - 2 * k, count)
+            sky_copy("inface", packed, sky, origin, sibling, pass_send, pass_recv, k).wait_recv()
+        for copy in sky_copies:
+            copy.wait_send()
     for e in range(blocks):
         span = span_map[0, e]
         owner, slot = span // blocks, span % blocks
@@ -140,17 +203,13 @@
     cosine_here = sun[0]
     slant = (-math.log2(math.e)) / jnp.where(cosine_here > 0.0, cosine_here, 1.0)
 
-    def optics(l, total):
-        step = (1.2 + jnp.tanh(state[l, field(1), :])) * slant
+    def descend(l, total):
+        step = depth[l] * slant
         depth[l] = step
         path[l] = total
         return total + step
 
-    if "optics" not in SKIP:
-        bottom = lax.fori_loop(0, levels, optics, jnp.zeros_like(slant), unroll=2)
-        path[levels] = bottom
-    else:
-        bottom = slant
+    path[levels] = lax.fori_loop(0, levels, descend, jnp.zeros_like(slant), unroll=2)
 
     shape = (8, LANES)
     for g in range(blocks // 8):
@@ -160,7 +219,7 @@
             total = total + weights[b] * jnp.exp2(absorb[b] * path[levels, rows, :])
         flux[rows, :] = (1.0 - sun[1, rows, :]) * sun[0, rows, :] * total
     fluxes[me] = flux[...]
-    flux_copies = exchange(count, "inface", flux, fluxes, send_sem.at[1], recv_sem.at[1]) if count > 1 else []
+    flux_copies = exchange(count, "inface", flux, fluxes, send_sem, recv_sem) if count > 1 else []
 
     for g in range(blocks // 8):
         rows = pl.ds(g * 8, 8)
@@ -207,14 +266,14 @@
             pltpu.make_async_copy(state.at[:, pl.ds(c * fields, fields), :], state_out.at[:, :, columns(c)], out_sem.at[0]).start()
 
     if count > 1:
-        finish(count, "inface", flux, fluxes, send_sem.at[1], recv_sem.at[1], flux_copies)
+        finish(count, "inface", flux, fluxes, send_sem, recv_sem, flux_copies)
     mine = (lax.broadcasted_iota(jnp.int32, (blocks, blocks), 0) + me * blocks).astype(jnp.float32)
     surface = jnp.zeros((blocks, LANES), jnp.float32)
     for r in range(count):
-        span_of = sky[r, pl.ds(2 * blocks, 1), pl.ds(0, blocks)]
+        span_of = fluxes[r, pl.ds(blocks, 1), pl.ds(0, blocks)]
         pick = jnp.where(mine == span_of, 1.0, 0.0)
         surface = surface + jnp.dot(
-            pick, fluxes[r], preferred_element_type=jnp.float32, precision=lax.Precision.HIGHEST
+            pick, fluxes[r, pl.ds(0, blocks), :], preferred_element_type=jnp.float32, precision=lax.Precision.HIGHEST
         )
     surface_out[...] = surface
     pltpu.make_async_copy(state, state, out_sem.at[0]).wait()
@@ -223,19 +282,23 @@
 def run_step(count, cosine, albedo, sunlit, span_map, absorb, weights, model_state, coupling):
     levels, fields, columns = model_state.shape
     blocks = columns // LANES
-    smem = pl.BlockSpec(memory_space=pltpu.SMEM)
+    operands = (cosine, albedo, sunlit, span_map, absorb, weights, model_state, coupling)
     vmem = pl.BlockSpec(memory_space=pltpu.VMEM)
     anywhere = pl.BlockSpec(memory_space=pl.ANY)
-    rows = 2 * blocks + 8
     return pl.pallas_call(
         functools.partial(step_kernel, count),
         out_shape=(
             jax.ShapeDtypeStruct(model_state.shape, jnp.float32),
             jax.ShapeDtypeStruct((blocks, LANES), jnp.float32),
         ),
-        in_specs=[vmem, vmem, smem, smem, vmem, smem, smem, anywhere, anywhere],
+        in_specs=[pl.BlockSpec(memory_space=pltpu.HBM)] * 8,
         out_specs=(anywhere, vmem),
         scratch_shapes=[
+            pltpu.VMEM(span_map.shape, jnp.int32),
+            pltpu.SMEM(sunlit.shape, jnp.int32),
+            pltpu.SMEM(span_map.shape, jnp.int32),
+            pltpu.SMEM(absorb.shape, jnp.float32),
+            pltpu.SMEM(weights.shape, jnp.float32),
             pltpu.VMEM((levels, blocks * fields, LANES), jnp.float32),
             pltpu.VMEM((fields, levels, blocks, LANES), jnp.float32),
             pltpu.VMEM((levels, blocks, LANES), jnp.float32),
@@ -243,20 +306,25 @@
             pltpu.VMEM((levels, blocks, LANES), jnp.float32),
             pltpu.VMEM((levels + 1, blocks, LANES), jnp.float32),
             pltpu.VMEM((2, blocks, LANES), jnp.float32),
-            pltpu.VMEM((rows, LANES), jnp.float32),
-            pltpu.VMEM((count, rows, LANES), jnp.float32),
-            pltpu.VMEM((blocks, LANES), jnp.float32),
-            pltpu.VMEM((count, blocks, LANES), jnp.float32),
+            pltpu.VMEM((2 * blocks, LANES), jnp.float32),
+            pltpu.VMEM((count, 2 * blocks, LANES), jnp.float32),
+            pltpu.VMEM((blocks + 8, LANES), jnp.float32),
+            pltpu.VMEM((count, blocks + 8, LANES), jnp.float32),
             pltpu.SemaphoreType.DMA((2,)),
+            pltpu.SemaphoreType.DMA((7,)),
             pltpu.SemaphoreType.DMA((1,)),
-            pltpu.SemaphoreType.DMA((2, max(count, 2))),
-            pltpu.SemaphoreType.DMA((2, max(count, 2))),
+            pltpu.SemaphoreType.DMA((max(count // 2, 1),)),
+            pltpu.SemaphoreType.DMA((max(count // 2, 1),)),
+            pltpu.SemaphoreType.DMA((max(count // 2, 1),)),
+            pltpu.SemaphoreType.DMA((max(count // 2, 1),)),
+            pltpu.SemaphoreType.DMA((count,)),
+            pltpu.SemaphoreType.DMA((count,)),
         ],
         compiler_params=pltpu.CompilerParams(
             collective_id=0 if count > 1 else None, has_side_effects=True, vmem_limit_bytes=40 * 1024 * 1024
         ),
         name="step",
-    )(cosine, albedo, sunlit, span_map, span_map, absorb, weights, model_state, coupling)
+    )(*(pltpu.with_memory_space_constraint(x, pltpu.HBM) for x in operands))
 
 
 def body(model_state, coupling, cosine, albedo, absorb, weights, span_map, sunlit):

time: 32.9 us -> 22.5 us (0.68)
  local copies, waits for them, and re-layouts: 9.83 us -> 2.49 us
  Pallas kernels: 21.9 us -> 19.2 us
    unnamed x18 -> x2, local copies, waits for them, and re-layouts: 9.83 us -> 2.49 us
    pallas_call x1, Pallas kernels: 21.9 us -> 19.2 us  [run_step(): pl.pallas_call(functools.partial(step_kernel, count), out_shape=(jax.Shap...]
where the time goes in v2:
time: 22.5 us; the launch traced here: 22.3 us
  Pallas kernels  19.2 us (85%)
  local copies, waits for them, and re-layouts  2.49 us (11%)
  between operations  0.64 us (3%)
    pallas_call x1, Pallas kernels, run_step(): pl.pallas_call(functools.partial(step_kernel, count), out_shape=(jax.Shap...  19.2 us
    unnamed x2, local copies, waits for them, and re-layouts  2.49 us

profile of v2, /device:TPU:0, one launch (start us, length us, event | category | flops | bytes accessed | tf_op | source)
XLA Modules:
  0.0 22.3 jit_solution(6079315787977040502)
XLA Ops:
  0.6 19.2 %step.1 = (f32[58,4,4096]{2,1,0:T(4,128)S(1)}, f32[32,128]{1,0:T(8,128)S(1)}) custom-call(f32[32,128]{1,0:T(8,128)} %bitcast.8, f32[32,128]{1,0:T(8,128)} %bitcast.9, s32[1,32]{1,0:T(1,128)} %sunlit_in.1, s32[1,32]{1,0:T(1,128)} %span_map_in.1, f32[14]{0:T(128)} %absorb_in.1, f32[14]{0:T(128)} %weights_in.1, f32[58,4,4096]{2,1,0:T(4,128)} %bitcast.7, ...), custom_call_target="tpu_custom_call" | custom-call | tf_op jit(solution)/shard_map/step/pallas_call | solution.py:288
  19.8 1.9 %copy.12 = f32[4,58,4096]{2,0,1:T(4,128)} copy(f32[4,58,4096]{2,0,1:T(4,128)S(1)} %bitcast.5) | data formatting | bytes 7602176
  21.7 0.6 %copy.13 = f32[4096]{0:T(1024)} copy(f32[4096]{0:T(1024)S(1)} %bitcast.6) | data formatting | bytes 32768

commit v3 on v2

--- a/solution.py
+++ b/solution.py
@@ -66,9 +66,6 @@
         device_id={axis: peer},
         device_id_type=MESH,
     )
-
-
-SKIP = ()
 
 
 def step_kernel(
@@ -107,11 +104,6 @@
     def field(f, first=0, size=blocks):
         return pl.ds(first * fields + f, size, stride=fields)
 
-    for c in range(blocks):
-        pltpu.make_async_copy(coupling_in.at[:, columns(c)], coupling.at[:, c, :], in_sem.at[0]).start()
-    for c in range(blocks):
-        pltpu.make_async_copy(state_in.at[:, :, columns(c)], state.at[:, pl.ds(c * fields, fields), :], in_sem.at[1]).start()
-
     for copy in small:
         copy.wait()
     for s in range(blocks):
@@ -130,48 +122,52 @@
         for copy in sky_copies:
             copy.start()
 
+    for c in range(blocks):
+        pltpu.make_async_copy(coupling_in.at[:, columns(c)], coupling.at[:, c, :], in_sem.at[0]).start()
+    for c in range(blocks):
+        pltpu.make_async_copy(state_in.at[:, :, columns(c)], state.at[:, pl.ds(c * fields, fields), :], in_sem.at[1]).start()
+
     pltpu.make_async_copy(coupling, coupling, in_sem.at[0]).wait()
     pltpu.make_async_copy(state, state, in_sem.at[1]).wait()
 
-    if "solve" not in SKIP:
-        below = coupling[0]
-        scale = 1.0 / (1.0 + below)
+    below = coupling[0]
+    scale = 1.0 / (1.0 + below)
+    gain_now = below * scale
+    gain[0] = gain_now
+    values = []
+    for f in range(fields):
+        value = state[0, field(f), :] * scale
+        partial[f, 0] = value
+        values.append(value)
+
+    def eliminate(l, carry):
+        above, gain_last, *last = carry
+        below = coupling[l]
+        scale = 1.0 / (1.0 + below + above - above * gain_last)
         gain_now = below * scale
-        gain[0] = gain_now
-        values = []
+        gain[l] = gain_now
+        now = []
         for f in range(fields):
-            value = state[0, field(f), :] * scale
-            partial[f, 0] = value
-            values.append(value)
-
-        def eliminate(l, carry):
-            above, gain_last, *last = carry
-            below = coupling[l]
-            scale = 1.0 / (1.0 + below + above - above * gain_last)
-            gain_now = below * scale
-            gain[l] = gain_now
-            now = []
-            for f in range(fields):
-                value = (state[l, field(f), :] + above * last[f]) * scale
-                partial[f, l] = value
-                now.append(value)
-            return (below, gain_now, *now)
-
-        carry = lax.fori_loop(1, levels, eliminate, (below, gain_now, *values), unroll=3)
+            value = (state[l, field(f), :] + above * last[f]) * scale
+            partial[f, l] = value
+            now.append(value)
+        return (below, gain_now, *now)
+
+    carry = lax.fori_loop(1, levels, eliminate, (below, gain_now, *values), unroll=8)
+    for f in range(fields):
+        state[levels - 1, field(f), :] = carry[2 + f]
+
+    def substitute(k, carry):
+        l = levels - 2 - k
+        g = gain[l]
+        now = []
         for f in range(fields):
-            state[levels - 1, field(f), :] = carry[2 + f]
-
-        def substitute(k, carry):
-            l = levels - 2 - k
-            g = gain[l]
-            now = []
-            for f in range(fields):
-                value = partial[f, l] + g * carry[f]
-                state[l, field(f), :] = value
-                now.append(value)
-            return tuple(now)
-
-        lax.fori_loop(0, levels - 1, substitute, tuple(carry[2:]), unroll=3)
+            value = partial[f, l] + g * carry[f]
+            state[l, field(f), :] = value
+            now.append(value)
+        return tuple(now)
+
+    lax.fori_loop(0, levels - 1, substitute, tuple(carry[2:]), unroll=8)
 
     if count > 1:
         for k in range(1, chips):
@@ -185,7 +181,7 @@
         depth[l] = 1.2 + jnp.tanh(state[l, field(1), :])
         return nothing
 
-    lax.fori_loop(0, levels, optics, 0, unroll=2)
+    lax.fori_loop(0, levels, optics, 0, unroll=8)
 
     if count > 1:
         sky_copy("inface", packed, sky, sibling, sibling, sky_send, sky_recv, 0).wait_recv()
@@ -209,7 +205,7 @@
         path[l] = total
         return total + step
 
-    path[levels] = lax.fori_loop(0, levels, descend, jnp.zeros_like(slant), unroll=2)
+    path[levels] = lax.fori_loop(0, levels, descend, jnp.zeros_like(slant), unroll=8)
 
     shape = (8, LANES)
     for g in range(blocks // 8):
@@ -260,21 +256,21 @@
             state[l, here, :] = state[l, here, :] + factor * (net_below - net)
             return (net, *now)
 
-        if "radiate" not in SKIP:
-            lax.fori_loop(0, levels, radiate, (net, *ups), unroll=2)
+        lax.fori_loop(0, levels, radiate, (net, *ups), unroll=29)
         for c in range(g * 8, g * 8 + 8):
             pltpu.make_async_copy(state.at[:, pl.ds(c * fields, fields), :], state_out.at[:, :, columns(c)], out_sem.at[0]).start()
 
     if count > 1:
         finish(count, "inface", flux, fluxes, send_sem, recv_sem, flux_copies)
-    mine = (lax.broadcasted_iota(jnp.int32, (blocks, blocks), 0) + me * blocks).astype(jnp.float32)
-    surface = jnp.zeros((blocks, LANES), jnp.float32)
-    for r in range(count):
-        span_of = fluxes[r, pl.ds(blocks, 1), pl.ds(0, blocks)]
-        pick = jnp.where(mine == span_of, 1.0, 0.0)
-        surface = surface + jnp.dot(
-            pick, fluxes[r, pl.ds(0, blocks), :], preferred_element_type=jnp.float32, precision=lax.Precision.HIGHEST
-        )
+    mine = (lax.broadcasted_iota(jnp.int32, (blocks, count * blocks), 0) + me * blocks).astype(jnp.float32)
+    span_of = jnp.concatenate([fluxes[r, pl.ds(blocks, 1), pl.ds(0, blocks)] for r in range(count)], axis=1)
+    every = jnp.concatenate([fluxes[r, pl.ds(0, blocks), :] for r in range(count)], axis=0)
+    surface = jnp.dot(
+        jnp.where(mine == span_of, 1.0, 0.0),
+        every,
+        preferred_element_type=jnp.float32,
+        precision=lax.Precision.HIGHEST,
+    )
     surface_out[...] = surface
     pltpu.make_async_copy(state, state, out_sem.at[0]).wait()
 

time: 22.5 us -> 20.8 us (0.924)
  Pallas kernels: 19.2 us -> 17.4 us
    pallas_call x1, Pallas kernels: 19.2 us -> 17.4 us  [run_step(): pl.pallas_call(functools.partial(step_kernel, count), out_shape=(jax.Shap...]
where the time goes in v3:
time: 20.8 us; the launch traced here: 20.5 us
  Pallas kernels  17.4 us (84%)
  local copies, waits for them, and re-layouts  2.49 us (12%)
  between operations  0.64 us (3%)
    pallas_call x1, Pallas kernels, run_step(): pl.pallas_call(functools.partial(step_kernel, count), out_shape=(jax.Shap...  17.4 us
    unnamed x2, local copies, waits for them, and re-layouts  2.49 us

profile of v3, /device:TPU:0, one launch (start us, length us, event | category | flops | bytes accessed | tf_op | source)
XLA Modules:
  0.0 20.5 jit_solution(14523431923860947976)
XLA Ops:
  0.6 17.4 %step.1 = (f32[58,4,4096]{2,1,0:T(4,128)S(1)}, f32[32,128]{1,0:T(8,128)S(1)}) custom-call(f32[32,128]{1,0:T(8,128)} %bitcast.8, f32[32,128]{1,0:T(8,128)} %bitcast.9, s32[1,32]{1,0:T(1,128)} %sunlit_in.1, s32[1,32]{1,0:T(1,128)} %span_map_in.1, f32[14]{0:T(128)} %absorb_in.1, f32[14]{0:T(128)} %weights_in.1, f32[58,4,4096]{2,1,0:T(4,128)} %bitcast.7, ...), custom_call_target="tpu_custom_call" | custom-call | tf_op jit(solution)/shard_map/step/pallas_call | solution.py:284
  18.0 1.9 %copy.12 = f32[4,58,4096]{2,0,1:T(4,128)} copy(f32[4,58,4096]{2,0,1:T(4,128)S(1)} %bitcast.5) | data formatting | bytes 7602176
  19.9 0.6 %copy.13 = f32[4096]{0:T(1024)} copy(f32[4096]{0:T(1024)S(1)} %bitcast.6) | data formatting | bytes 32768

commit v4 on v3

--- a/solution.py
+++ b/solution.py
@@ -104,6 +104,11 @@
     def field(f, first=0, size=blocks):
         return pl.ds(first * fields + f, size, stride=fields)
 
+    for c in range(blocks):
+        pltpu.make_async_copy(coupling_in.at[:, columns(c)], coupling.at[:, c, :], in_sem.at[0]).start()
+    for c in range(blocks):
+        pltpu.make_async_copy(state_in.at[:, :, columns(c)], state.at[:, pl.ds(c * fields, fields), :], in_sem.at[1]).start()
+
     for copy in small:
         copy.wait()
     for s in range(blocks):
@@ -121,11 +126,6 @@
         sky_copies.append(sky_copy("inface", packed, sky, me, sibling, sky_send, sky_recv, 0))
         for copy in sky_copies:
             copy.start()
-
-    for c in range(blocks):
-        pltpu.make_async_copy(coupling_in.at[:, columns(c)], coupling.at[:, c, :], in_sem.at[0]).start()
-    for c in range(blocks):
-        pltpu.make_async_copy(state_in.at[:, :, columns(c)], state.at[:, pl.ds(c * fields, fields), :], in_sem.at[1]).start()
 
     pltpu.make_async_copy(coupling, coupling, in_sem.at[0]).wait()
     pltpu.make_async_copy(state, state, in_sem.at[1]).wait()

time: 20.8 us -> 20.6 us (level)
  no operation moved by 1% of the time
where the time goes in v4:
time: 20.6 us; the launch traced here: 20.4 us
  Pallas kernels  17.2 us (83%)
  local copies, waits for them, and re-layouts  2.49 us (12%)
  between operations  0.64 us (3%)
    pallas_call x1, Pallas kernels, run_step(): pl.pallas_call(functools.partial(step_kernel, count), out_shape=(jax.Shap...  17.2 us
    unnamed x2, local copies, waits for them, and re-layouts  2.49 us

profile of v4, /device:TPU:0, one launch (start us, length us, event | category | flops | bytes accessed | tf_op | source)
XLA Modules:
  0.0 20.4 jit_solution(8098589799839624686)
XLA Ops:
  0.6 17.2 %step.1 = (f32[58,4,4096]{2,1,0:T(4,128)S(1)}, f32[32,128]{1,0:T(8,128)S(1)}) custom-call(f32[32,128]{1,0:T(8,128)} %bitcast.8, f32[32,128]{1,0:T(8,128)} %bitcast.9, s32[1,32]{1,0:T(1,128)} %sunlit_in.1, s32[1,32]{1,0:T(1,128)} %span_map_in.1, f32[14]{0:T(128)} %absorb_in.1, f32[14]{0:T(128)} %weights_in.1, f32[58,4,4096]{2,1,0:T(4,128)} %bitcast.7, ...), custom_call_target="tpu_custom_call" | custom-call | tf_op jit(solution)/shard_map/step/pallas_call | solution.py:284
  17.9 1.9 %copy.12 = f32[4,58,4096]{2,0,1:T(4,128)} copy(f32[4,58,4096]{2,0,1:T(4,128)S(1)} %bitcast.5) | data formatting | bytes 7602176
  19.8 0.6 %copy.13 = f32[4096]{0:T(1024)} copy(f32[4096]{0:T(1024)S(1)} %bitcast.6) | data formatting | bytes 32768
